TPU v7x, 256 devices: a whole 4x4x8 slice. The times are simulated.
256 devices in a mesh: dp: 16 (over x, y_hi, core), seq: 16 (over y_lo, z).
Axes of the slice: x: 4, y: 4 (y_hi: 2, y_lo: 2; y = y_hi * 2 + y_lo), z: 8, core: 2. Of those that a mesh axis runs over, the one named last changes fastest.
Arguments:
- encoder_input: bfloat16 [16, 2048, 1536], P('dp'), may hold values from -6 to 6
- sublayer_norm_gain: float32 [1536], replicated, may hold values from 0.25 to 1.75
- sublayer_norm_bias: float32 [1536], replicated, may hold values from -3 to 3
- gate_up_weight: bfloat16 [2, 1536, 4096], P(None, None, 'seq'), may hold values from -0.15625 to 0.15625
- down_weight: bfloat16 [4096, 1536], P('seq'), may hold values from -0.09375 to 0.09375
- branch_layer_scale: float32 [1536], replicated, may hold values from 0.3 to 1
- closing_norm_gain: float32 [1536], replicated, may hold values from 0.25 to 1.75
- closing_norm_bias: float32 [1536], replicated, may hold values from -3 to 3
- diffusion_hidden: bfloat16 [16, 2048, 2048], P('dp', 'seq'), may hold values from -6 to 6
- projector_weight: bfloat16 [2048, 1536], P(('dp', 'seq')), may hold values from -0.125 to 0.125
Outputs:
- hidden_gradient: bfloat16 [16, 2048, 2048], P('dp', 'seq')
- grad_weight: float32 [2048, 1536], P(('dp', 'seq'))
All inputs are finite; a program needn't handle non-finite values.
Results may differ from a plain program's by a relative error of at most 0.02.
Values may be sent and summed in bfloat16 or wider, within the bound.
A program may use at most 128 MiB of HBM per device.

v0:
```python
import jax
import jax.numpy as jnp
from jax import lax
from jax.sharding import PartitionSpec as P


def layer_norm(values, gain, shift):
    mean = jnp.mean(values, axis=-1, keepdims=True)
    centered = values - mean
    var = jnp.mean(centered * centered, axis=-1, keepdims=True)
    return centered / jnp.sqrt(var + 1e-06) * gain + shift


def on_device(
    encoder_input,
    sublayer_norm_gain,
    sublayer_norm_bias,
    gate_up_weight,
    down_weight,
    branch_layer_scale,
    closing_norm_gain,
    closing_norm_bias,
    diffusion_hidden,
    projector_weight,
):
    full_weight = lax.all_gather(projector_weight, ("dp", "seq"), axis=0, tiled=True)
    token_rows = diffusion_hidden.shape[1]
    shard = lax.axis_index("seq")
    inputs = encoder_input[0].astype(jnp.float32)
    normed = layer_norm(inputs, sublayer_norm_gain, sublayer_norm_bias).astype(jnp.bfloat16)
    gate = jnp.dot(normed, gate_up_weight[0], preferred_element_type=jnp.float32)
    up = jnp.dot(normed, gate_up_weight[1], preferred_element_type=jnp.float32)
    hidden = (jax.nn.silu(gate) * up).astype(jnp.bfloat16)
    own_inputs = lax.dynamic_slice_in_dim(inputs, shard * token_rows, token_rows, 0)
    branch = lax.psum_scatter(
        jnp.dot(hidden, down_weight, preferred_element_type=jnp.float32)
        .astype(jnp.bfloat16)
        .astype(jnp.float32)
        .astype(jnp.bfloat16),
        "seq",
        scatter_dimension=0,
        tiled=True,
    ).astype(jnp.float32)
    target = layer_norm(
        own_inputs + branch_layer_scale * branch, closing_norm_gain, closing_norm_bias
    )
    width = full_weight.shape[1]
    token_count = diffusion_hidden[0]
    pred = jnp.dot(token_count, full_weight, preferred_element_type=jnp.float32)
    pred_norm = jnp.sqrt(jnp.sum(pred * pred, axis=-1, keepdims=True) + 1e-06)
    target_norm = jnp.sqrt(jnp.sum(target * target, axis=-1, keepdims=True) + 1e-06)
    cosine = jnp.sum(pred * target, axis=-1, keepdims=True) / (pred_norm * target_norm)
    grad_pred = (
        -1.0
        * width
        * (target / (pred_norm * target_norm) - cosine * pred / (pred_norm * pred_norm))
    )
    grad_pred = grad_pred.astype(jnp.bfloat16)
    hidden_gradient = lax.dot_general(
        grad_pred, full_weight, (((1,), (1,)), ((), ())), preferred_element_type=jnp.float32
    )
    hidden_gradient = hidden_gradient.astype(jnp.bfloat16)[None]
    grand_sum = lax.axis_size("dp") * encoder_input.shape[1]
    factor = 1.0 / jnp.sqrt(jnp.float32(grand_sum))
    grad_weight = lax.psum_scatter(
        lax.dot_general(
            token_count, grad_pred, (((0,), (0,)), ((), ())), preferred_element_type=jnp.float32
        )
        * factor,
        ("dp", "seq"),
        scatter_dimension=0,
        tiled=True,
    )
    return (hidden_gradient, grad_weight)


def solution(mesh):
    in_specs = (
        P("dp", None, None),
        P(),
        P(),
        P(None, None, "seq"),
        P("seq", None),
        P(),
        P(),
        P(),
        P("dp", "seq", None),
        P(("dp", "seq"), None),
    )
    out_specs = (P("dp", "seq", None), P(("dp", "seq"), None))
    return jax.shard_map(
        on_device, mesh=mesh, in_specs=in_specs, out_specs=out_specs, check_vma=False
    )
```

profile of v0, /device:TPU:1, one launch (start us, length us, event | category | flops | bytes accessed | tf_op | source)
XLA Modules:
  0.0 2066.6 jit_solution(14383132840913174295)
XLA Ops:
  8.0 0.0 copy-start
  8.0 0.0 copy-start.6
  8.0 0.0 copy-start.7
  8.0 0.0 reduce-scatter.5.cloned.1.call-start
  8.1 0.0 copy-start.2
  8.1 3.8 convert_reduce_fusion
  11.9 0.8 copy-done.2
  12.7 1.8 fusion.1
  14.5 0.0 copy-done.6
  14.6 0.0 copy-done.7
  14.6 0.0 copy-start.8
  14.6 9.0 fusion.2
  23.6 0.0 copy-start.3
  23.6 2.7 copy-done.3
  26.3 0.0 copy-done.8
  26.3 3.2 fusion.8
  29.5 0.0 copy-done
  29.5 12.3 convolution_convert_fusion
  41.8 0.0 reduce-scatter.5.cloned.1.call-update
  41.8 0.0 all-gather.2.cloned.1.call-start
  41.9 0.5 all-gather.2.cloned.1.call-update
  42.4 0.2 reduce-scatter.7.cloned.1.call-start
  42.7 0.0 copy-start.5
  42.7 0.0 copy-start.4
  42.7 0.0 copy-start.9
  42.7 0.0 copy-start.10
  42.7 9.2 convert_element_type.32
  51.9 72.5 %reduce-scatter.5.cloned.1.call-done = bf16[128,1536]{1,0:T(8,128)(2,1)} async-done(((bf16[2048,1536]{1,0:T(8,128)(2,1)}), bf16[128,1536]{1,0:T(8,128)(2,1)}) %reduce-scatter.5.cloned.1.call-update) | async-done | bytes 393232 | tf_op jit(solution)/shard_map/reduce_scatter | solution.py:35
  124.4 0.0 copy-done.5
  124.4 1.4 fusion.16
  125.9 1.5 multiply_reduce_fusion.3
  127.4 652.1 %all-gather.2.cloned.1.call-done = bf16[2048,1536]{1,0:T(8,128)(2,1)} async-done(((bf16[8,1536]{1,0:T(8,128)(2,1)}), bf16[2048,1536]{1,0:T(8,128)(2,1)}) %all-gather.2.cloned.1.call-update) | async-done | bytes 6291472 | tf_op jit(solution)/shard_map/all_gather | solution.py:26
  779.5 0.0 copy-done.4
  779.5 0.0 copy-done.9
  779.5 0.0 copy-done.10
  779.5 4.2 multiply_reduce_fusion.1
  783.8 6.4 multiply_bitcast_fusion
  790.2 12.6 copy.14
  802.8 0.0 reduce-scatter.7.cloned.1.call-update
  802.8 0.0 copy-start.1
  802.8 5.8 fusion.4
  808.6 1250.5 %reduce-scatter.7.cloned.1.call-done = f32[8,1536]{1,0:T(8,128)} async-done(((f32[2048,1536]{1,0:T(8,128)}), f32[8,1536]{1,0:T(8,128)}) %reduce-scatter.7.cloned.1.call-update) | async-done | bytes 49168
  2059.1 0.0 copy-done.1
  (5 shorter events, 0.0 us)
Async XLA Ops:
  8.0 21.5 %copy-start = (bf16[256,1536]{1,0:T(8,128)(2,1)S(1)}, bf16[256,1536]{1,0:T(8,128)(2,1)}, u32[]{:S(2)}) copy-start(bf16[256,1536]{1,0:T(8,128)(2,1)} %param.14) | copy-start | bytes 2359300
  8.0 6.5 copy-start.6
  8.0 6.5 copy-start.7
  8.0 116.4 %reduce-scatter.5.cloned.1.call-start = ((), (), s32[]{:S(2)}) async-start(), calls=%async_computation.2 | async-start | bytes 6684672 | tf_op jit(solution)/shard_map/reduce_scatter | solution.py:35
  8.1 4.7 copy-start.2
  14.6 11.7 copy-start.8
  23.6 2.7 copy-start.3
  41.8 737.7 %all-gather.2.cloned.1.call-start = ((), (), s32[]{:S(2)}) async-start(), calls=%async_computation.3 | async-start | bytes 6316032 | tf_op jit(solution)/shard_map/all_gather | solution.py:26
  42.4 2016.7 %reduce-scatter.7.cloned.1.call-start = ((), (), s32[]{:S(2)}) async-start(), calls=%async_computation.4 | async-start | bytes 12632064
  42.7 81.8 %copy-start.5 = (f32[1536]{0:T(1024)S(1)}, f32[1536]{0:T(1024)}, u32[]{:S(2)}) copy-start(f32[1536]{0:T(1024)} %param.15) | copy-start | bytes 18436
  42.7 736.9 %copy-start.4 = (bf16[1,128,2048]{2,1,0:T(8,128)(2,1)S(1)}, bf16[1,128,2048]{2,1,0:T(8,128)(2,1)}, u32[]{:S(2)}) copy-start(bf16[1,128,2048]{2,1,0:T(8,128)(2,1)} %param.18) | copy-start | bytes 1572868
  42.7 736.9 %copy-start.9 = (f32[1536]{0:T(1024)S(1)}, f32[1536]{0:T(1024)}, u32[]{:S(2)}) copy-start(f32[1536]{0:T(1024)} %param.17) | copy-start | bytes 18436
  42.7 736.8 %copy-start.10 = (f32[1536]{0:T(1024)S(1)}, f32[1536]{0:T(1024)}, u32[]{:S(2)}) copy-start(f32[1536]{0:T(1024)} %param.16) | copy-start | bytes 18436
  802.8 1256.3 %copy-start.1 = (bf16[256,1536]{1,0:T(8,128)(2,1)S(1)}, bf16[256,1536]{1,0:T(8,128)(2,1)}, u32[]{:S(2)}) copy-start(bf16[256,1536]{1,0:T(8,128)(2,1)} %param.14) | copy-start | bytes 2359300
Sparse Core Ops, SparseCore 0:
  42.0 82.4 reduce-scatter.4
Sparse Core Ops, SparseCore 1:
  44.2 735.3 all-gather.1
  802.9 1256.2 reduce-scatter.6
where the time goes:
time: 2100 us; the launch traced here: 2070 us
  waiting for transfers between devices  1980 us (94%)
  matrix products  32 us (2%)
  other arithmetic  26.8 us (1%)
    unnamed x4, waiting for transfers between devices  1250 us
    all_gather x1, waiting for transfers between devices, on_device(): lax.all_gather(projector_weight, ('dp', 'seq'), axis=0, tiled=True)  652 us
    reduce_scatter x1, waiting for transfers between devices, on_device(): lax.psum_scatter(jnp.dot(hidden, down_weight, preferred_element_type=jnp....  72.5 us
  transfers between devices with their start and end apart: 3, of which 3 were waited for; matrix products, arithmetic and copies ran while one was open for 1% of the time, Pallas kernels for 0%

commit v1 on v0

v1 whole, which is shorter than its diff:
```python
import functools

import jax
import jax.numpy as jnp
from jax import lax
from jax.experimental import pallas as pl
from jax.experimental.pallas import tpu as pltpu
from jax.sharding import PartitionSpec as P

F32 = jnp.float32
BF16 = jnp.bfloat16
EPS = 1e-06
TOKENS = 128
HALF_TOKENS = 1024
E = 1536
H = 768
Q = 384
WIDTH = 2048
HID = 256
SEMS = 128


def kernel(
    x_hbm, g1_ref, b1_ref, gu_hbm, dn_hbm, ls_ref, g2_ref, b2_ref, dh_hbm, pw_ref,
    hg_ref, gw_ref,
    xin, nrm, guo, dno, gux, dnx, hid, part, rz, w32, w, dh, dho, dht, pred,
    gp, gpall, ga, gb, ra, rb, sa, sb, ra2, rb2, s3, r3, res, fin,
    ssem, rsem, lsem,
):
    dp, seq = lax.axis_index("dp"), lax.axis_index("seq")
    x, yh, c = dp // 4, (dp // 2) % 2, dp % 2
    yl, z = seq // 8, seq % 8
    y = yh * 2 + yl

    def dev(xx, yy, zz, cc):
        return ((xx * 2 + yy // 2) * 2 + cc, (yy % 2) * 8 + zz)

    xp, xm, x2 = (x + 1) % 4, (x + 3) % 4, (x + 2) % 4
    yp, ym, y2 = (y + 1) % 4, (y + 3) % 4, (y + 2) % 4
    d_xp, d_xm = dev(xp, y, z, c), dev(xm, y, z, c)
    d_yp, d_ym = dev(x, yp, z, c), dev(x, ym, z, c)
    d_z = [None] + [dev(x, y, (z + k) % 8, c) for k in range(1, 8)]
    d_co = dev(x, y, z, 1 - c)

    barrier = pltpu.get_barrier_semaphore()
    peers = [d_xp, d_xm, d_yp, d_ym, d_co] + d_z[1:]
    for peer in peers:
        pl.semaphore_signal(barrier, inc=1, device_id=peer, device_id_type=pl.DeviceIdType.MESH)
    count = [0]
    sent = []

    def send(src, dst, device):
        k = count[0]
        count[0] += 1
        copy = pltpu.make_async_remote_copy(
            src_ref=src, dst_ref=dst, send_sem=ssem.at[k], recv_sem=rsem.at[k],
            device_id=device, device_id_type=pl.DeviceIdType.MESH,
        )
        copy.start()
        sent.append(copy)
        return copy

    def local(k, src, dst):
        copy = pltpu.make_async_copy(src, dst, lsem.at[k])
        copy.start()
        return copy

    c_x = local(0, x_hbm.at[pl.ds(pl.multiple_of(yl * HALF_TOKENS, HALF_TOKENS), HALF_TOKENS), :], xin)
    c_gu = local(1, gu_hbm, guo)
    c_dn = local(2, dn_hbm, dno)
    c_dh = local(3, dh_hbm, dh)
    w32[z] = pw_ref[...].astype(F32)
    pl.semaphore_wait(barrier, len(peers))

    def quarter(ref, side, core, size, lead):
        rows = pl.ds(pl.multiple_of((2 * side + core) * size, size), size)
        return ref.at[:, rows, :] if lead else ref.at[rows, :]

    f_gu = [send(quarter(gu_hbm, s, c, 384, True), quarter(gux, s, c, 384, True), d)
            for s, d in ((0, d_yp), (1, d_ym))]
    f_dn = [send(quarter(dn_hbm, s, c, 64, False), quarter(dnx, s, c, 64, False), d)
            for s, d in ((0, d_yp), (1, d_ym))]
    w_z = [send(w32.at[z], w32.at[z], d_z[k]) for k in (4, 3, 5, 2, 6, 1, 7)]
    c_dho = send(dh_hbm, dho, d_co)

    c_x.wait()
    gain1, bias1 = g1_ref[...].reshape(1, E), b1_ref[...].reshape(1, E)

    @pl.loop(0, HALF_TOKENS // 32)
    def _(i):
        rows = pl.ds(pl.multiple_of(i * 32, 32), 32)
        v = xin[rows, :].astype(F32)
        v = v - jnp.mean(v, axis=-1, keepdims=True)
        var = jnp.mean(v * v, axis=-1, keepdims=True)
        nrm[rows, :] = (v * lax.rsqrt(var + EPS) * gain1 + bias1).astype(BF16)

    def swish(values, weights):
        gate = jnp.dot(values, weights[0], preferred_element_type=F32)
        up = jnp.dot(values, weights[1], preferred_element_type=F32)
        return (gate * jax.nn.sigmoid(gate) * up).astype(BF16)

    c_gu.wait()

    @pl.loop(0, 4)
    def _(i):
        rows = pl.ds(pl.multiple_of(i * 256, 256), 256)
        hid[rows, :] = swish(nrm[rows, :], guo)

    for copy in w_z:
        copy.wait_recv()
    w[x, yh, c, yl] = w32[...].reshape(64, E).astype(BF16)
    col_a, col_b = pl.ds(0, H), pl.ds(H, H)
    a_l, a_r, b_l, b_r = (pl.ds(k * Q, Q) for k in range(4))

    def block(xx, yy, cols):
        return w.at[xx, yy // 2, c, yy % 2, :, cols]

    wa1 = [send(block(x, y, col_a), block(x, y, col_a), d) for d in (d_xp, d_xm)]
    wb1 = [send(block(x, y, col_b), block(x, y, col_b), d) for d in (d_yp, d_ym)]

    forwards = []
    for s, copy in ((0, f_gu[0]), (1, f_gu[1])):
        copy.wait_recv()
        piece = quarter(gux, s, c, 384, True)
        forwards.append(send(piece, piece, d_co))
    wa1[0].wait_recv()
    wa1r = [send(block(xm, y, a_l), block(xm, y, a_l), d_xp)]
    wa1[1].wait_recv()
    wa1r.append(send(block(xp, y, a_r), block(xp, y, a_r), d_xm))
    for s, copy in ((0, f_dn[0]), (1, f_dn[1])):
        copy.wait_recv()
        piece = quarter(dnx, s, c, 64, False)
        forwards.append(send(piece, piece, d_co))
    for copy in wa1r:
        copy.wait_recv()

    def column(yy, cols):
        return w.at[:, yy // 2, c, yy % 2, :, cols]

    def slab(xx, cols):
        return w.at[xx, :, c, :, :, cols]

    wa2 = [send(column(y, col_a), column(y, col_a), d) for d in (d_yp, d_ym)]
    c_dn.wait()
    for copy in forwards:
        copy.wait_recv()

    def ffn(ca, cb):
        ra_ = pl.ds(pl.multiple_of(ca * TOKENS, TOKENS), TOKENS)
        rb_ = pl.ds(pl.multiple_of(cb * TOKENS, TOKENS), TOKENS)
        values = jnp.concatenate([nrm[ra_, :], nrm[rb_, :]], axis=0)
        own = jnp.concatenate([hid[ra_, :], hid[rb_, :]], axis=0)
        other = swish(values, gux)
        for n in range(4):
            cols = pl.ds(n * Q, Q)
            out = jnp.dot(own, dno[:, cols], preferred_element_type=F32)
            out += jnp.dot(other, dnx[:, cols], preferred_element_type=F32)
            out = out.astype(BF16)
            cols = pl.ds((n % 2) * Q, Q)
            part[ca, n // 2, :, cols] = out[:TOKENS]
            part[cb, n // 2, :, cols] = out[TOKENS:]

    subs = [pl.ds(0, 64), pl.ds(64, 64)]
    ffn((z + 7) % 8, (z + 1) % 8)
    ring = []
    for sub in subs:
        ring.append([
            send(part.at[(z + 7) % 8, 0, sub, :], rz.at[0, 0, sub, :], d_z[1]),
            send(part.at[(z + 1) % 8, 1, sub, :], rz.at[1, 0, sub, :], d_z[7]),
        ])

    @pl.loop(1, 4)
    def _(j):
        ffn((z + 7 - j) % 8, (z + (j + 1) % 4) % 8)

    def ring_step(s):
        following = []
        for k, sub in enumerate(subs):
            pair = []
            for d in range(2):
                ring[k][d].wait_recv()
                chunk = (z + 6 - s) % 8 if d == 0 else (z + 2 + s) % 8
                total = rz[d, s, sub, :].astype(F32) + part[chunk, d, sub, :].astype(F32)
                rz[d, s, sub, :] = total.astype(BF16)
                pair.append(send(rz.at[d, s, sub, :], rz.at[d, s + 1, sub, :], d_z[1] if d == 0 else d_z[7]))
            following.append(pair)
        ring[:] = following

    ring_step(0)
    wb1[0].wait_recv()
    wb1r = [send(block(x, ym, b_l), block(x, ym, b_l), d_yp)]
    wb1[1].wait_recv()
    wb1r.append(send(block(x, yp, b_r), block(x, yp, b_r), d_ym))
    for copy in wb1r:
        copy.wait_recv()
    wb2 = [send(slab(x, col_b), slab(x, col_b), d) for d in (d_xp, d_xm)]
    ring_step(1)
    c_dh.wait()
    c_dho.wait_recv()

    @pl.loop(0, 4)
    def _(xx):
        for k in range(4):
            cols = pl.ds(pl.multiple_of(xx * 512 + k * 128, 128), 128)
            for t, ref in enumerate((dh, dho)):
                turned = ref[:, cols].T
                for low in range(2):
                    dht[xx, (k // 2) * 2 + low, pl.ds((k % 2) * 64, 64), pl.ds(t * 128, 128)] = (
                        turned[low * 64:(low + 1) * 64]
                    )

    ring_step(2)
    wa2[0].wait_recv()
    wa2r = [send(column(ym, a_l), column(ym, a_l), d_yp)]
    wa2[1].wait_recv()
    wa2r.append(send(column(yp, a_r), column(yp, a_r), d_ym))
    wb2[0].wait_recv()
    wb2r = [send(slab(xm, b_l), slab(xm, b_l), d_xp)]
    wb2[1].wait_recv()
    wb2r.append(send(slab(xp, b_r), slab(xp, b_r), d_xm))
    ring_step(3)
    ring_step(4)
    for copy in wa2r + wb2r:
        copy.wait_recv()
    w_co = send(w.at[:, :, c], w.at[:, :, c], d_co)
    ring_step(5)
    w_co.wait_recv()

    @pl.loop(0, 3)
    def _(n):
        cols = pl.ds(pl.multiple_of(n * 512, 512), 512)
        total = jnp.zeros((TOKENS, 512), F32)
        for k in range(4):
            total += jnp.dot(
                dh[:, pl.ds(k * 512, 512)], w[k, :, :, :, :, cols].reshape(512, 512),
                preferred_element_type=F32,
            )
        pred[:, cols] = total

    for k in range(2):
        for d in range(2):
            ring[k][d].wait_recv()
    scale, gain2, bias2 = (r[...].reshape(1, E) for r in (ls_ref, g2_ref, b2_ref))

    @pl.loop(0, TOKENS // 16)
    def _(i):
        rows = pl.ds(pl.multiple_of(i * 16, 16), 16)
        branch = jnp.concatenate(
            [part[z, d, rows, :].astype(F32) + rz[d, 6, rows, :].astype(F32) for d in range(2)], axis=1
        )
        own_rows = pl.ds(pl.multiple_of(z * TOKENS + i * 16, 16), 16)
        v = xin[own_rows, :].astype(F32) + scale * branch
        v = v - jnp.mean(v, axis=-1, keepdims=True)
        var = jnp.mean(v * v, axis=-1, keepdims=True)
        t = v * lax.rsqrt(var + EPS) * gain2 + bias2
        p = pred[rows, :]
        inv_p = lax.rsqrt(jnp.sum(p * p, axis=-1, keepdims=True) + EPS)
        inv_t = lax.rsqrt(jnp.sum(t * t, axis=-1, keepdims=True) + EPS)
        dot = jnp.sum(p * t, axis=-1, keepdims=True)
        lead = (-1.0 * E) * (inv_p * inv_t)
        grad = (lead * (t - (dot * inv_p * inv_p) * p)).astype(BF16)
        gp[0, rows, :] = grad[:, :H]
        gp[1, rows, :] = grad[:, H:]

    c_gp = send(gp.at[1 - c], gpall.at[pl.ds(128, 128), :], d_co)
    gpall[pl.ds(0, 128), :] = gp[c]
    c_gp.wait_recv()

    def grad_slab(xx):
        out = jnp.dot(dht[xx].reshape(512, 256), gpall[...], preferred_element_type=F32).astype(BF16)
        for half in range(2):
            ga[xx, half] = out[half * 256:(half + 1) * 256, :Q]
        for yy in range(4):
            gb[yy, xx // 2, pl.ds(pl.multiple_of((xx % 2) * 128, 128), 128), :] = (
                out[yy * 128:(yy + 1) * 128, Q:]
            )

    def first(g, r, two, plus, minus, dplus, dminus):
        return dict(
            l2=send(g.at[two, 0], r.at[0], dplus), r2=send(g.at[two, 1], r.at[3], dminus),
        )

    def second(o, g, r, plus, minus, dplus, dminus):
        o["ro"] = send(g.at[plus, 1], r.at[1], dplus)
        o["lo"] = send(g.at[minus, 0], r.at[4], dminus)

    def relay(o, g, r, plus, minus, dplus, dminus):
        o["l2"].wait_recv()
        r[0] = (r[0].astype(F32) + g[plus, 0].astype(F32)).astype(BF16)
        o["ls"] = send(r.at[0], r.at[2], dplus)
        o["r2"].wait_recv()
        r[3] = (r[3].astype(F32) + g[minus, 1].astype(F32)).astype(BF16)
        o["rs"] = send(r.at[3], r.at[5], dminus)

    def total(o, g, r, me):
        for name in ("ro", "lo", "ls", "rs"):
            o[name].wait_recv()
        left = g[me, 0].astype(F32) + r[2].astype(F32) + r[4].astype(F32)
        right = g[me, 1].astype(F32) + r[1].astype(F32) + r[5].astype(F32)
        return left, right

    on_x, on_y = (xp, xm, d_xp, d_xm), (yp, ym, d_yp, d_ym)
    grad_slab(x2)
    oa = first(ga, ra, x2, *on_x)
    grad_slab(xp)
    grad_slab(xm)
    second(oa, ga, ra, *on_x)
    grad_slab(x)
    ob = first(gb, rb, y2, *on_y)
    second(ob, gb, rb, *on_y)

    def hidden_gradient(k):
        rows = w.at[k]
        out = jnp.zeros((TOKENS, 512), F32)
        for d in range(2):
            out += lax.dot_general(
                gp[d], rows[:, :, :, :, pl.ds(d * H, H)].reshape(512, H),
                (((1,), (1,)), ((), ())), preferred_element_type=F32,
            )
        hg_ref[0, :, pl.ds(pl.multiple_of(k * 512, 512), 512)] = out.astype(BF16)

    @pl.loop(0, 2)
    def _(k):
        hidden_gradient(k)

    relay(oa, ga, ra, *on_x)
    relay(ob, gb, rb, *on_y)

    @pl.loop(2, 4)
    def _(k):
        hidden_gradient(k)

    left, right = total(oa, ga, ra, x)
    for k, half in enumerate((left, right)):
        half = half.astype(BF16)
        for q in range(4):
            sa[2 * k + q // 2, q % 2] = half[q * 64:(q + 1) * 64]
    oa2 = first(sa, ra2, y2, *on_y)
    second(oa2, sa, ra2, *on_y)
    left, right = total(ob, gb, rb, y)
    for k, half in enumerate((left, right)):
        half = half.astype(BF16)
        for q in range(4):
            sb[2 * k + q // 2, q % 2] = half[q * 64:(q + 1) * 64]
    ob2 = first(sb, rb2, x2, *on_x)
    second(ob2, sb, rb2, *on_x)
    relay(oa2, sa, ra2, *on_y)
    relay(ob2, sb, rb2, *on_x)
    for k, (o, s, r, me) in enumerate(((oa2, sa, ra2, y), (ob2, sb, rb2, x))):
        left, right = total(o, s, r, me)
        both = jnp.concatenate([left.reshape(8, 8, Q), right.reshape(8, 8, Q)], axis=1)
        s3[:, :, pl.ds(k * Q, Q)] = both.astype(BF16)
    last = [send(s3.at[(z + k) % 8], r3.at[z], d_z[k]) for k in (4, 3, 5, 2, 6, 1, 7)]
    r3[z] = s3[z]
    for copy in last:
        copy.wait_recv()
    tot = jnp.sum(r3[...].astype(F32), axis=0) * (1.0 / (16 * 2048) ** 0.5)
    res[0] = tot[:8]
    res[1] = tot[8:]
    c_fin = send(res.at[1 - c], fin, d_co)
    gw_ref[:, pl.ds(pl.multiple_of(c * H, H), H)] = res[c]
    for copy in sent[:-1]:
        copy.wait_send()
    c_fin.wait_recv()
    gw_ref[:, pl.ds(pl.multiple_of((1 - c) * H, H), H)] = fin[...]
    c_fin.wait_send()


def on_device(
    encoder_input, sublayer_norm_gain, sublayer_norm_bias, gate_up_weight, down_weight,
    branch_layer_scale, closing_norm_gain, closing_norm_bias, diffusion_hidden, projector_weight,
):
    hbm = pl.BlockSpec(memory_space=pl.ANY)
    vmem = pl.BlockSpec(memory_space=pltpu.VMEM)
    return pl.pallas_call(
        kernel,
        out_shape=(
            jax.ShapeDtypeStruct((1, TOKENS, WIDTH), BF16),
            jax.ShapeDtypeStruct((8, E), F32),
        ),
        in_specs=[hbm, vmem, vmem, hbm, hbm, vmem, vmem, vmem, hbm, vmem],
        out_specs=(vmem, vmem),
        scratch_shapes=[
            pltpu.VMEM((HALF_TOKENS, E), BF16),
            pltpu.VMEM((HALF_TOKENS, E), BF16),
            pltpu.VMEM((2, E, HID), BF16),
            pltpu.VMEM((HID, E), BF16),
            pltpu.VMEM((2, E, HID), BF16),
            pltpu.VMEM((HID, E), BF16),
            pltpu.VMEM((HALF_TOKENS, HID), BF16),
            pltpu.VMEM((8, 2, TOKENS, H), BF16),
            pltpu.VMEM((2, 7, TOKENS, H), BF16),
            pltpu.VMEM((8, 8, E), F32),
            pltpu.VMEM((4, 2, 2, 2, 64, E), BF16),
            pltpu.VMEM((TOKENS, WIDTH), BF16),
            pltpu.VMEM((TOKENS, WIDTH), BF16),
            pltpu.VMEM((4, 4, 128, 256), BF16),
            pltpu.VMEM((TOKENS, E), F32),
            pltpu.VMEM((2, TOKENS, H), BF16),
            pltpu.VMEM((256, H), BF16),
            pltpu.VMEM((4, 2, 256, Q), BF16),
            pltpu.VMEM((4, 2, 256, Q), BF16),
            pltpu.VMEM((6, 256, Q), BF16),
            pltpu.VMEM((6, 256, Q), BF16),
            pltpu.VMEM((4, 2, 64, Q), BF16),
            pltpu.VMEM((4, 2, 64, Q), BF16),
            pltpu.VMEM((6, 64, Q), BF16),
            pltpu.VMEM((6, 64, Q), BF16),
            pltpu.VMEM((8, 16, H), BF16),
            pltpu.VMEM((8, 16, H), BF16),
            pltpu.VMEM((2, 8, H), F32),
            pltpu.VMEM((8, H), F32),
            pltpu.SemaphoreType.DMA((SEMS,)),
            pltpu.SemaphoreType.DMA((SEMS,)),
            pltpu.SemaphoreType.DMA((4,)),
        ],
        compiler_params=pltpu.CompilerParams(
            collective_id=0, has_side_effects=True, vmem_limit_bytes=56 * 1024 * 1024
        ),
    )(
        encoder_input[0], sublayer_norm_gain, sublayer_norm_bias, gate_up_weight, down_weight,
        branch_layer_scale, closing_norm_gain, closing_norm_bias, diffusion_hidden[0], projector_weight,
    )


def solution(mesh):
    in_specs = (
        P("dp", None, None), P(), P(), P(None, None, "seq"), P("seq", None), P(), P(), P(),
        P("dp", "seq", None), P(("dp", "seq"), None),
    )
    out_specs = (P("dp", "seq", None), P(("dp", "seq"), None))
    return jax.shard_map(
        on_device, mesh=mesh, in_specs=in_specs, out_specs=out_specs, check_vma=False
    )
```

time: 2100 us -> 108 us (0.05); the launches traced: 2070 us -> 108 us
  waiting for transfers between devices: 1980 us -> 0 us
  Pallas kernels: 0 us -> 104 us
  matrix products: 32 us -> 0 us
  other arithmetic: 26.8 us -> 0 us
    unnamed x4 -> x0, waiting for transfers between devices: 1250 us -> none
    all_gather x1 -> x0, waiting for transfers between devices: 652 us -> none  [on_device(): lax.all_gather(projector_weight, ('dp', 'seq'), axis=0, tiled=True)]
    pallas_call x0 -> x1, Pallas kernels: none -> 104 us  [on_device(): pl.pallas_call(kernel, out_shape=(jax.ShapeDtypeStruct((1, TOKENS, WIDTH)...]
    reduce_scatter x1 -> x0, waiting for transfers between devices: 72.5 us -> none  [on_device(): lax.psum_scatter(jnp.dot(hidden, down_weight, preferred_element_type=jnp....]
    dot_general x5 -> x0, matrix products: 32 us -> none  [the longest x1 12.3 us: on_device(): jnp.dot(hidden, down_weight, preferred_element_type=jnp.float32)]
  transfers between devices with their start and end apart: 3 -> 0, of which waited for: 3 -> 0; matrix products, arithmetic and copies ran while one was open for 1% -> 0% of each run, Pallas kernels for 0% -> 0%
where the time goes in v1:
time: 108 us
  Pallas kernels  104 us (96%)
  local copies, waits for them, and re-layouts  3.3 us (3%)
    pallas_call x1, Pallas kernels, on_device(): pl.pallas_call(kernel, out_shape=(jax.ShapeDtypeStruct((1, TOKENS, WIDTH)...  104 us
    unnamed x2, local copies, waits for them, and re-layouts  3.3 us

profile of v1, /device:TPU:1, one launch (start us, length us, event | category | flops | bytes accessed | tf_op | source)
XLA Modules:
  0.0 107.7 jit_solution(13952642341484621424)
XLA Ops:
  0.6 103.8 %shard_map.113 = (bf16[1,128,2048]{2,1,0:T(8,128)(2,1)}, f32[8,1536]{1,0:T(8,128)}) custom-call(bf16[2048,1536]{1,0:T(8,128)(2,1)} %bitcast.2, f32[1536]{0:T(1024)} %g1_ref.1, f32[1536]{0:T(1024)} %b1_ref.1, bf16[2,1536,256]{2,1,0:T(8,128)(2,1)} %gu_hbm.1, bf16[256,1536]{1,0:T(8,128)(2,1)} %dn_hbm.1, f32[1536]{0:T(1024)} %ls_ref.1, f32[1536]{0:T(1024)} %g2_ref.1, ...), custom_call_target="tpu_custom_call" | custom-call | tf_op jit(solution)/shard_map/pallas_call | solution.py:375
  104.4 1.9 %copy.14 = bf16[1,128,2048]{2,1,0:T(8,128)(2,1)} copy(bf16[1,128,2048]{2,1,0:T(8,128)(2,1)} %get-tuple-element.4) | data formatting | bytes 1048576
  106.3 1.4 %copy.15 = f32[8,1536]{1,0:T(8,128)} copy(f32[8,1536]{1,0:T(8,128)} %get-tuple-element.5) | data formatting | bytes 98304

commit v2 on v1

--- a/solution.py
+++ b/solution.py
@@ -11,19 +11,20 @@
 BF16 = jnp.bfloat16
 EPS = 1e-06
 TOKENS = 128
-HALF_TOKENS = 1024
+EARLY = 32
+LATE = 96
 E = 1536
 H = 768
 Q = 384
 WIDTH = 2048
 HID = 256
-SEMS = 128
+SEMS = 160
 
 
 def kernel(
     x_hbm, g1_ref, b1_ref, gu_hbm, dn_hbm, ls_ref, g2_ref, b2_ref, dh_hbm, pw_ref,
     hg_ref, gw_ref,
-    xin, nrm, guo, dno, gux, dnx, hid, part, rz, w32, w, dh, dho, dht, pred,
+    xs, xl, ns, nl, guo, dno, gux, dnx, hl, ep, re, es, ex, lp, rl, wu, w, dh, dho, dht, pred,
     gp, gpall, ga, gb, ra, rb, sa, sb, ra2, rb2, s3, r3, res, fin,
     ssem, rsem, lsem,
 ):
@@ -41,6 +42,7 @@
     d_yp, d_ym = dev(x, yp, z, c), dev(x, ym, z, c)
     d_z = [None] + [dev(x, y, (z + k) % 8, c) for k in range(1, 8)]
     d_co = dev(x, y, z, 1 - c)
+    d_pair = dev(x, yh * 2 + 1 - yl, z, c)
 
     barrier = pltpu.get_barrier_semaphore()
     peers = [d_xp, d_xm, d_yp, d_ym, d_co] + d_z[1:]
@@ -65,11 +67,36 @@
         copy.start()
         return copy
 
-    c_x = local(0, x_hbm.at[pl.ds(pl.multiple_of(yl * HALF_TOKENS, HALF_TOKENS), HALF_TOKENS), :], xin)
+    c_xs = local(0, x_hbm.at[:, pl.ds(0, EARLY), :], xs)
     c_gu = local(1, gu_hbm, guo)
     c_dn = local(2, dn_hbm, dno)
-    c_dh = local(3, dh_hbm, dh)
-    w32[z] = pw_ref[...].astype(F32)
+    c_xl = local(3, x_hbm.at[pl.ds(yl * 8, 8), pl.ds(EARLY, LATE), :], xl)
+    c_dh = local(4, dh_hbm, dh)
+    rows_w = pw_ref[...].astype(F32)
+    wu[z] = jnp.concatenate([rows_w[:, :H], rows_w[:, H:]], axis=0).astype(BF16)
+    gain1, bias1 = g1_ref[...].reshape(1, E), b1_ref[...].reshape(1, E)
+
+    def norm(v):
+        v = v.astype(F32)
+        v = v - jnp.mean(v, axis=-1, keepdims=True)
+        var = jnp.mean(v * v, axis=-1, keepdims=True)
+        return (v * lax.rsqrt(var + EPS) * gain1 + bias1).astype(BF16)
+
+    def swish(values, weights):
+        gate = jnp.dot(values, weights[0], preferred_element_type=F32)
+        up = jnp.dot(values, weights[1], preferred_element_type=F32)
+        return (gate * jax.nn.sigmoid(gate) * up).astype(BF16)
+
+    def chunks(j):
+        return (z + 7 - j) % 8, (z + (j + 1) % 4) % 8
+
+    def norm_early(j):
+        for chunk in chunks(j):
+            ns[chunk, pl.ds(0, EARLY), :] = norm(xs[yl * 8 + chunk])
+            ns[chunk, pl.ds(EARLY, EARLY), :] = norm(xs[(1 - yl) * 8 + chunk])
+
+    c_xs.wait()
+    norm_early(0)
     pl.semaphore_wait(barrier, len(peers))
 
     def quarter(ref, side, core, size, lead):
@@ -80,121 +107,162 @@
             for s, d in ((0, d_yp), (1, d_ym))]
     f_dn = [send(quarter(dn_hbm, s, c, 64, False), quarter(dnx, s, c, 64, False), d)
             for s, d in ((0, d_yp), (1, d_ym))]
-    w_z = [send(w32.at[z], w32.at[z], d_z[k]) for k in (4, 3, 5, 2, 6, 1, 7)]
+
+    def unit(k):
+        return wu.at[(z + k) % 8]
+
+    wz = [send(unit(0), unit(0), d_z[1]), send(unit(0), unit(0), d_z[7])]
     c_dho = send(dh_hbm, dho, d_co)
 
-    c_x.wait()
-    gain1, bias1 = g1_ref[...].reshape(1, E), b1_ref[...].reshape(1, E)
-
-    @pl.loop(0, HALF_TOKENS // 32)
-    def _(i):
-        rows = pl.ds(pl.multiple_of(i * 32, 32), 32)
-        v = xin[rows, :].astype(F32)
-        v = v - jnp.mean(v, axis=-1, keepdims=True)
-        var = jnp.mean(v * v, axis=-1, keepdims=True)
-        nrm[rows, :] = (v * lax.rsqrt(var + EPS) * gain1 + bias1).astype(BF16)
-
-    def swish(values, weights):
-        gate = jnp.dot(values, weights[0], preferred_element_type=F32)
-        up = jnp.dot(values, weights[1], preferred_element_type=F32)
-        return (gate * jax.nn.sigmoid(gate) * up).astype(BF16)
-
+    def ffn_early(j):
+        ca, cb = chunks(j)
+        hidden = swish(jnp.concatenate([ns[ca], ns[cb]], axis=0), guo)
+        for n in range(4):
+            out = jnp.dot(hidden, dno[:, pl.ds(n * Q, Q)], preferred_element_type=F32).astype(BF16)
+            cols = pl.ds((n % 2) * Q, Q)
+            ep[ca, n // 2, :, cols] = out[:64]
+            ep[cb, n // 2, :, cols] = out[64:]
+
+    def ring_start(p, r, subs):
+        return [[
+            send(p.at[(z + 7) % 8, 0, sub, :], r.at[0, 0, sub, :], d_z[1]),
+            send(p.at[(z + 1) % 8, 1, sub, :], r.at[1, 0, sub, :], d_z[7]),
+        ] for sub in subs]
+
+    def ring_step(s, ring, p, r, subs):
+        following = []
+        for k, sub in enumerate(subs):
+            pair = []
+            for d in range(2):
+                ring[k][d].wait_recv()
+                chunk = (z + 6 - s) % 8 if d == 0 else (z + 2 + s) % 8
+                both = r[d, s, sub, :].astype(F32) + p[chunk, d, sub, :].astype(F32)
+                r[d, s, sub, :] = both.astype(BF16)
+                pair.append(send(r.at[d, s, sub, :], r.at[d, s + 1, sub, :], d_z[1] if d == 0 else d_z[7]))
+            following.append(pair)
+        ring[:] = following
+
+    e_subs = [pl.ds(0, EARLY), pl.ds(EARLY, EARLY)]
+    l_subs = [pl.ds(0, 48), pl.ds(48, 48)]
     c_gu.wait()
-
-    @pl.loop(0, 4)
-    def _(i):
-        rows = pl.ds(pl.multiple_of(i * 256, 256), 256)
-        hid[rows, :] = swish(nrm[rows, :], guo)
-
-    for copy in w_z:
-        copy.wait_recv()
-    w[x, yh, c, yl] = w32[...].reshape(64, E).astype(BF16)
+    c_dn.wait()
+    ffn_early(0)
+    e_ring = ring_start(ep, re, e_subs)
+    norm_early(1)
+    ffn_early(1)
+    for copy in wz:
+        copy.wait_recv()
+    wz = [send(unit(7), unit(7), d_z[1]), send(unit(1), unit(1), d_z[7])]
+    ring_step(0, e_ring, ep, re, e_subs)
+    norm_early(2)
+    ffn_early(2)
+    for copy in wz:
+        copy.wait_recv()
+    wz = [send(unit(6), unit(6), d_z[1]), send(unit(2), unit(2), d_z[7])]
+    ring_step(1, e_ring, ep, re, e_subs)
+    norm_early(3)
+    ffn_early(3)
+    for copy in wz:
+        copy.wait_recv()
+    wz = [send(unit(5), unit(5), d_z[1])]
+    ring_step(2, e_ring, ep, re, e_subs)
+
+    def prepare_late(j):
+        for chunk in chunks(j):
+            @pl.loop(0, LATE // 32)
+            def _(i):
+                rows = pl.ds(pl.multiple_of(i * 32, 32), 32)
+                nl[chunk, rows, :] = norm(xl[chunk, rows, :])
+
+        ca, cb = chunks(j)
+        hidden = swish(jnp.concatenate([nl[ca], nl[cb]], axis=0), guo)
+        hl[ca] = hidden[:LATE]
+        hl[cb] = hidden[LATE:]
+
+    c_xl.wait()
+    prepare_late(0)
+    wz[0].wait_recv()
+    units = wu[...].astype(F32)
+    w[x, yh, c, yl, :, pl.ds(0, H)] = units[:, :8].reshape(64, H).astype(BF16)
+    w[x, yh, c, yl, :, pl.ds(H, H)] = units[:, 8:].reshape(64, H).astype(BF16)
     col_a, col_b = pl.ds(0, H), pl.ds(H, H)
     a_l, a_r, b_l, b_r = (pl.ds(k * Q, Q) for k in range(4))
 
     def block(xx, yy, cols):
         return w.at[xx, yy // 2, c, yy % 2, :, cols]
 
-    wa1 = [send(block(x, y, col_a), block(x, y, col_a), d) for d in (d_xp, d_xm)]
-    wb1 = [send(block(x, y, col_b), block(x, y, col_b), d) for d in (d_yp, d_ym)]
-
+    def column(yy, cols):
+        return w.at[:, yy // 2, c, yy % 2, :, cols]
+
+    def slab(xx, cols):
+        return w.at[xx, :, c, :, :, cols]
+
+    def core_half(cols):
+        return w.at[:, :, c, :, :, cols]
+
+    def same(piece, device):
+        return send(piece, piece, device)
+
+    wa1 = [same(block(x, y, col_a), d) for d in (d_xp, d_xm)]
+    wb1 = [same(block(x, y, col_b), d) for d in (d_yp, d_ym)]
+    ring_step(3, e_ring, ep, re, e_subs)
+    prepare_late(1)
+    wa1[0].wait_recv()
+    wa1r = [same(block(xm, y, a_l), d_xp)]
+    wa1[1].wait_recv()
+    wa1r.append(same(block(xp, y, a_r), d_xm))
     forwards = []
     for s, copy in ((0, f_gu[0]), (1, f_gu[1])):
         copy.wait_recv()
-        piece = quarter(gux, s, c, 384, True)
-        forwards.append(send(piece, piece, d_co))
-    wa1[0].wait_recv()
-    wa1r = [send(block(xm, y, a_l), block(xm, y, a_l), d_xp)]
-    wa1[1].wait_recv()
-    wa1r.append(send(block(xp, y, a_r), block(xp, y, a_r), d_xm))
+        forwards.append(same(quarter(gux, s, c, 384, True), d_co))
+    ring_step(4, e_ring, ep, re, e_subs)
+    prepare_late(2)
+    for copy in wa1r:
+        copy.wait_recv()
+    wa2 = [same(column(y, col_a), d) for d in (d_yp, d_ym)]
+    ring_step(5, e_ring, ep, re, e_subs)
+    prepare_late(3)
     for s, copy in ((0, f_dn[0]), (1, f_dn[1])):
         copy.wait_recv()
-        piece = quarter(dnx, s, c, 64, False)
-        forwards.append(send(piece, piece, d_co))
-    for copy in wa1r:
-        copy.wait_recv()
-
-    def column(yy, cols):
-        return w.at[:, yy // 2, c, yy % 2, :, cols]
-
-    def slab(xx, cols):
-        return w.at[xx, :, c, :, :, cols]
-
-    wa2 = [send(column(y, col_a), column(y, col_a), d) for d in (d_yp, d_ym)]
-    c_dn.wait()
+        forwards.append(same(quarter(dnx, s, c, 64, False), d_co))
     for copy in forwards:
         copy.wait_recv()
 
-    def ffn(ca, cb):
-        ra_ = pl.ds(pl.multiple_of(ca * TOKENS, TOKENS), TOKENS)
-        rb_ = pl.ds(pl.multiple_of(cb * TOKENS, TOKENS), TOKENS)
-        values = jnp.concatenate([nrm[ra_, :], nrm[rb_, :]], axis=0)
-        own = jnp.concatenate([hid[ra_, :], hid[rb_, :]], axis=0)
-        other = swish(values, gux)
+    def ffn_late(j):
+        ca, cb = chunks(j)
+        other = swish(jnp.concatenate([nl[ca], nl[cb]], axis=0), gux)
+        own = jnp.concatenate([hl[ca], hl[cb]], axis=0)
         for n in range(4):
             cols = pl.ds(n * Q, Q)
             out = jnp.dot(own, dno[:, cols], preferred_element_type=F32)
             out += jnp.dot(other, dnx[:, cols], preferred_element_type=F32)
             out = out.astype(BF16)
             cols = pl.ds((n % 2) * Q, Q)
-            part[ca, n // 2, :, cols] = out[:TOKENS]
-            part[cb, n // 2, :, cols] = out[TOKENS:]
-
-    subs = [pl.ds(0, 64), pl.ds(64, 64)]
-    ffn((z + 7) % 8, (z + 1) % 8)
-    ring = []
-    for sub in subs:
-        ring.append([
-            send(part.at[(z + 7) % 8, 0, sub, :], rz.at[0, 0, sub, :], d_z[1]),
-            send(part.at[(z + 1) % 8, 1, sub, :], rz.at[1, 0, sub, :], d_z[7]),
-        ])
-
-    @pl.loop(1, 4)
+            lp[ca, n // 2, :, cols] = out[:LATE]
+            lp[cb, n // 2, :, cols] = out[LATE:]
+
+    ffn_late(0)
+    l_ring = ring_start(lp, rl, l_subs)
+    for pair in e_ring:
+        for copy in pair:
+            copy.wait_recv()
+    for d in range(2):
+        es[d] = (re[d, 6, e_subs[1], :].astype(F32) + ep[z, d, e_subs[1], :].astype(F32)).astype(BF16)
+    c_ex = send(es, ex, d_pair)
+    wb1[0].wait_recv()
+    wb1r = [same(block(x, ym, b_l), d_yp)]
+    wb1[1].wait_recv()
+    wb1r.append(same(block(x, yp, b_r), d_ym))
+
+    @pl.loop(1, 3)
     def _(j):
-        ffn((z + 7 - j) % 8, (z + (j + 1) % 4) % 8)
-
-    def ring_step(s):
-        following = []
-        for k, sub in enumerate(subs):
-            pair = []
-            for d in range(2):
-                ring[k][d].wait_recv()
-                chunk = (z + 6 - s) % 8 if d == 0 else (z + 2 + s) % 8
-                total = rz[d, s, sub, :].astype(F32) + part[chunk, d, sub, :].astype(F32)
-                rz[d, s, sub, :] = total.astype(BF16)
-                pair.append(send(rz.at[d, s, sub, :], rz.at[d, s + 1, sub, :], d_z[1] if d == 0 else d_z[7]))
-            following.append(pair)
-        ring[:] = following
-
-    ring_step(0)
-    wb1[0].wait_recv()
-    wb1r = [send(block(x, ym, b_l), block(x, ym, b_l), d_yp)]
-    wb1[1].wait_recv()
-    wb1r.append(send(block(x, yp, b_r), block(x, yp, b_r), d_ym))
+        ffn_late(j)
+
     for copy in wb1r:
         copy.wait_recv()
-    wb2 = [send(slab(x, col_b), slab(x, col_b), d) for d in (d_xp, d_xm)]
-    ring_step(1)
+    wb2 = [same(slab(x, col_b), d) for d in (d_xp, d_xm)]
+    ffn_late(3)
+    ring_step(0, l_ring, lp, rl, l_subs)
     c_dh.wait()
     c_dho.wait_recv()
 
@@ -209,47 +277,43 @@
                         turned[low * 64:(low + 1) * 64]
                     )
 
-    ring_step(2)
+    ring_step(1, l_ring, lp, rl, l_subs)
     wa2[0].wait_recv()
-    wa2r = [send(column(ym, a_l), column(ym, a_l), d_yp)]
+    wa2r = [same(column(ym, a_l), d_yp)]
     wa2[1].wait_recv()
-    wa2r.append(send(column(yp, a_r), column(yp, a_r), d_ym))
+    wa2r.append(same(column(yp, a_r), d_ym))
+    ring_step(2, l_ring, lp, rl, l_subs)
     wb2[0].wait_recv()
-    wb2r = [send(slab(xm, b_l), slab(xm, b_l), d_xp)]
+    wb2r = [same(slab(xm, b_l), d_xp)]
     wb2[1].wait_recv()
-    wb2r.append(send(slab(xp, b_r), slab(xp, b_r), d_xm))
-    ring_step(3)
-    ring_step(4)
-    for copy in wa2r + wb2r:
-        copy.wait_recv()
-    w_co = send(w.at[:, :, c], w.at[:, :, c], d_co)
-    ring_step(5)
-    w_co.wait_recv()
+    wb2r.append(same(slab(xp, b_r), d_xm))
+    ring_step(3, l_ring, lp, rl, l_subs)
+    for copy in wa2r:
+        copy.wait_recv()
+    w_co = [same(core_half(col_a), d_co)]
+    ring_step(4, l_ring, lp, rl, l_subs)
+    for copy in wb2r:
+        copy.wait_recv()
+    w_co.append(same(core_half(col_b), d_co))
+    ring_step(5, l_ring, lp, rl, l_subs)
+    for copy in w_co:
+        copy.wait_recv()
 
     @pl.loop(0, 3)
     def _(n):
         cols = pl.ds(pl.multiple_of(n * 512, 512), 512)
-        total = jnp.zeros((TOKENS, 512), F32)
+        acc = jnp.zeros((TOKENS, 512), F32)
         for k in range(4):
-            total += jnp.dot(
+            acc += jnp.dot(
                 dh[:, pl.ds(k * 512, 512)], w[k, :, :, :, :, cols].reshape(512, 512),
                 preferred_element_type=F32,
             )
-        pred[:, cols] = total
-
-    for k in range(2):
-        for d in range(2):
-            ring[k][d].wait_recv()
+        pred[:, cols] = acc
+
     scale, gain2, bias2 = (r[...].reshape(1, E) for r in (ls_ref, g2_ref, b2_ref))
 
-    @pl.loop(0, TOKENS // 16)
-    def _(i):
-        rows = pl.ds(pl.multiple_of(i * 16, 16), 16)
-        branch = jnp.concatenate(
-            [part[z, d, rows, :].astype(F32) + rz[d, 6, rows, :].astype(F32) for d in range(2)], axis=1
-        )
-        own_rows = pl.ds(pl.multiple_of(z * TOKENS + i * 16, 16), 16)
-        v = xin[own_rows, :].astype(F32) + scale * branch
+    def loss_gradient(own, branch, rows):
+        v = own.astype(F32) + scale * jnp.concatenate(branch, axis=1)
         v = v - jnp.mean(v, axis=-1, keepdims=True)
         var = jnp.mean(v * v, axis=-1, keepdims=True)
         t = v * lax.rsqrt(var + EPS) * gain2 + bias2
@@ -262,9 +326,35 @@
         gp[0, rows, :] = grad[:, :H]
         gp[1, rows, :] = grad[:, H:]
 
-    c_gp = send(gp.at[1 - c], gpall.at[pl.ds(128, 128), :], d_co)
-    gpall[pl.ds(0, 128), :] = gp[c]
-    c_gp.wait_recv()
+    def swap_gradient(start, size):
+        gpall[pl.ds(start, size), :] = gp[c, pl.ds(start, size), :]
+        return send(gp.at[1 - c, pl.ds(start, size), :], gpall.at[pl.ds(128 + start, size), :], d_co)
+
+    c_ex.wait_recv()
+
+    @pl.loop(0, EARLY // 16)
+    def _(i):
+        rows = pl.ds(pl.multiple_of(i * 16, 16), 16)
+        branch = [
+            ep[z, d, rows, :].astype(F32) + re[d, 6, rows, :].astype(F32) + ex[d, rows, :].astype(F32)
+            for d in range(2)
+        ]
+        loss_gradient(xs[yl * 8 + z, rows, :], branch, rows)
+
+    c_gp = [swap_gradient(0, EARLY)]
+    for k in range(2):
+        for d in range(2):
+            l_ring[k][d].wait_recv()
+
+        @pl.loop(3 * k, 3 * k + 3)
+        def _(i):
+            rows = pl.ds(pl.multiple_of(i * 16, 16), 16)
+            branch = [lp[z, d, rows, :].astype(F32) + rl[d, 6, rows, :].astype(F32) for d in range(2)]
+            loss_gradient(xl[z, rows, :], branch, pl.ds(pl.multiple_of(EARLY + i * 16, 16), 16))
+
+        c_gp.append(swap_gradient(EARLY + 48 * k, 48))
+    for copy in c_gp:
+        copy.wait_recv()
 
     def grad_slab(xx):
         out = jnp.dot(dht[xx].reshape(512, 256), gpall[...], preferred_element_type=F32).astype(BF16)
@@ -381,16 +471,22 @@
         in_specs=[hbm, vmem, vmem, hbm, hbm, vmem, vmem, vmem, hbm, vmem],
         out_specs=(vmem, vmem),
         scratch_shapes=[
-            pltpu.VMEM((HALF_TOKENS, E), BF16),
-            pltpu.VMEM((HALF_TOKENS, E), BF16),
+            pltpu.VMEM((16, EARLY, E), BF16),
+            pltpu.VMEM((8, LATE, E), BF16),
+            pltpu.VMEM((8, 2 * EARLY, E), BF16),
+            pltpu.VMEM((8, LATE, E), BF16),
             pltpu.VMEM((2, E, HID), BF16),
             pltpu.VMEM((HID, E), BF16),
             pltpu.VMEM((2, E, HID), BF16),
             pltpu.VMEM((HID, E), BF16),
-            pltpu.VMEM((HALF_TOKENS, HID), BF16),
-            pltpu.VMEM((8, 2, TOKENS, H), BF16),
-            pltpu.VMEM((2, 7, TOKENS, H), BF16),
-            pltpu.VMEM((8, 8, E), F32),
+            pltpu.VMEM((8, LATE, HID), BF16),
+            pltpu.VMEM((8, 2, 2 * EARLY, H), BF16),
+            pltpu.VMEM((2, 7, 2 * EARLY, H), BF16),
+            pltpu.VMEM((2, EARLY, H), BF16),
+            pltpu.VMEM((2, EARLY, H), BF16),
+            pltpu.VMEM((8, 2, LATE, H), BF16),
+            pltpu.VMEM((2, 7, LATE, H), BF16),
+            pltpu.VMEM((8, 16, H), BF16),
             pltpu.VMEM((4, 2, 2, 2, 64, E), BF16),
             pltpu.VMEM((TOKENS, WIDTH), BF16),
             pltpu.VMEM((TOKENS, WIDTH), BF16),
@@ -412,13 +508,13 @@
             pltpu.VMEM((8, H), F32),
             pltpu.SemaphoreType.DMA((SEMS,)),
             pltpu.SemaphoreType.DMA((SEMS,)),
-            pltpu.SemaphoreType.DMA((4,)),
+            pltpu.SemaphoreType.DMA((5,)),
         ],
         compiler_params=pltpu.CompilerParams(
             collective_id=0, has_side_effects=True, vmem_limit_bytes=56 * 1024 * 1024
         ),
     )(
-        encoder_input[0], sublayer_norm_gain, sublayer_norm_bias, gate_up_weight, down_weight,
+        encoder_input[0].reshape(16, TOKENS, E), sublayer_norm_gain, sublayer_norm_bias, gate_up_weight, down_weight,
         branch_layer_scale, closing_norm_gain, closing_norm_bias, diffusion_hidden[0], projector_weight,
     )
 

time: 108 us -> 111 us (1.028)
  Pallas kernels: 104 us -> 107 us
    pallas_call x1, Pallas kernels: 104 us -> 107 us  [on_device(): pl.pallas_call(kernel, out_shape=(jax.ShapeDtypeStruct((1, TOKENS, WIDTH)...]
where the time goes in v2:
time: 111 us
  Pallas kernels  107 us (96%)
  local copies, waits for them, and re-layouts  3.3 us (3%)
    pallas_call x1, Pallas kernels, on_device(): pl.pallas_call(kernel, out_shape=(jax.ShapeDtypeStruct((1, TOKENS, WIDTH)...  107 us
    unnamed x2, local copies, waits for them, and re-layouts  3.3 us

profile of v2, /device:TPU:1, one launch (start us, length us, event | category | flops | bytes accessed | tf_op | source)
XLA Modules:
  0.0 110.9 jit_solution(13390961019092172584)
XLA Ops:
  0.6 107.0 %shard_map.113 = (bf16[1,128,2048]{2,1,0:T(8,128)(2,1)}, f32[8,1536]{1,0:T(8,128)}) custom-call(bf16[16,128,1536]{2,1,0:T(8,128)(2,1)} %bitcast.2, f32[1536]{0:T(1024)} %g1_ref.1, f32[1536]{0:T(1024)} %b1_ref.1, bf16[2,1536,256]{2,1,0:T(8,128)(2,1)} %gu_hbm.1, bf16[256,1536]{1,0:T(8,128)(2,1)} %dn_hbm.1, f32[1536]{0:T(1024)} %ls_ref.1, f32[1536]{0:T(1024)} %g2_ref.1, ...), custom_call_target="tpu_custom_call" | custom-call | tf_op jit(solution)/shard_map/pallas_call | solution.py:465
  107.6 1.9 %copy.14 = bf16[1,128,2048]{2,1,0:T(8,128)(2,1)} copy(bf16[1,128,2048]{2,1,0:T(8,128)(2,1)} %get-tuple-element.4) | data formatting | bytes 1048576
  109.5 1.4 %copy.15 = f32[8,1536]{1,0:T(8,128)} copy(f32[8,1536]{1,0:T(8,128)} %get-tuple-element.5) | data formatting | bytes 98304

commit v3 on v2

--- a/solution.py
+++ b/solution.py
@@ -18,7 +18,7 @@
 Q = 384
 WIDTH = 2048
 HID = 256
-SEMS = 160
+SEMS = 200
 
 
 def kernel(
@@ -88,7 +88,7 @@
         return (gate * jax.nn.sigmoid(gate) * up).astype(BF16)
 
     def chunks(j):
-        return (z + 7 - j) % 8, (z + (j + 1) % 4) % 8
+        return (z + 4 - j) % 8, (z + 4 + j) % 8 if not isinstance(j, int) or j else z
 
     def norm_early(j):
         for chunk in chunks(j):
@@ -99,20 +99,35 @@
     norm_early(0)
     pl.semaphore_wait(barrier, len(peers))
 
-    def quarter(ref, side, core, size, lead):
-        rows = pl.ds(pl.multiple_of((2 * side + core) * size, size), size)
-        return ref.at[:, rows, :] if lead else ref.at[rows, :]
-
-    f_gu = [send(quarter(gu_hbm, s, c, 384, True), quarter(gux, s, c, 384, True), d)
-            for s, d in ((0, d_yp), (1, d_ym))]
-    f_dn = [send(quarter(dn_hbm, s, c, 64, False), quarter(dnx, s, c, 64, False), d)
-            for s, d in ((0, d_yp), (1, d_ym))]
+    def piece(refs, side, core, k):
+        if k < 4:
+            return refs[0].at[:, pl.ds(pl.multiple_of((2 * side + core) * 384 + k * 96, 96), 96), :]
+        return refs[1].at[pl.ds(pl.multiple_of((2 * side + core) * 64 + (k - 4) * 32, 32), 32), :]
+
+    fetched, forwards = {}, []
+
+    def fetch(*ks):
+        for k in ks:
+            fetched[k] = [
+                send(piece((gu_hbm, dn_hbm), s, c, k), piece((gux, dnx), s, c, k), d)
+                for s, d in ((0, d_yp), (1, d_ym))
+            ]
+
+    def forward(*ks):
+        for k in ks:
+            for s, copy in enumerate(fetched[k]):
+                copy.wait_recv()
+                forwards.append(same(piece((gux, dnx), s, c, k), d_co))
+
+    def same(ref, device):
+        return send(ref, ref, device)
+
+    fetch(0, 1, 2)
 
     def unit(k):
         return wu.at[(z + k) % 8]
 
     wz = [send(unit(0), unit(0), d_z[1]), send(unit(0), unit(0), d_z[7])]
-    c_dho = send(dh_hbm, dho, d_co)
 
     def ffn_early(j):
         ca, cb = chunks(j)
@@ -123,49 +138,59 @@
             ep[ca, n // 2, :, cols] = out[:64]
             ep[cb, n // 2, :, cols] = out[64:]
 
-    def ring_start(p, r, subs):
-        return [[
-            send(p.at[(z + 7) % 8, 0, sub, :], r.at[0, 0, sub, :], d_z[1]),
-            send(p.at[(z + 1) % 8, 1, sub, :], r.at[1, 0, sub, :], d_z[7]),
-        ] for sub in subs]
-
-    def ring_step(s, ring, p, r, subs):
+
+    def ring_chunk(flow, hops):
+        return (z + hops) % 8 if flow == 0 else (z + 8 - hops) % 8
+
+    def ring_begin(p, r, far):
+        slot, hops = (0, 4) if far else (4, 3)
+        return [
+            send(p.at[ring_chunk(f, hops), f if far else 1 - f], r.at[f, slot], d_z[1 if f == 0 else 7])
+            for f in range(2)
+        ]
+
+    def ring_next(copies, p, r, slot, hops, far, subs=None):
         following = []
-        for k, sub in enumerate(subs):
-            pair = []
-            for d in range(2):
-                ring[k][d].wait_recv()
-                chunk = (z + 6 - s) % 8 if d == 0 else (z + 2 + s) % 8
-                both = r[d, s, sub, :].astype(F32) + p[chunk, d, sub, :].astype(F32)
-                r[d, s, sub, :] = both.astype(BF16)
-                pair.append(send(r.at[d, s, sub, :], r.at[d, s + 1, sub, :], d_z[1] if d == 0 else d_z[7]))
-            following.append(pair)
-        ring[:] = following
-
-    e_subs = [pl.ds(0, EARLY), pl.ds(EARLY, EARLY)]
+        for f in range(2):
+            copies[f].wait_recv()
+            half = f if far else 1 - f
+            for sub in subs or [slice(None)]:
+                both = r[f, slot, sub, :].astype(F32) + p[ring_chunk(f, hops), half, sub, :].astype(F32)
+                r[f, slot, sub, :] = both.astype(BF16)
+                src, dst = (r.at[f, slot], r.at[f, slot + 1]) if subs is None else (
+                    r.at[f, slot, sub, :], r.at[f, slot + 1, sub, :])
+                following.append(send(src, dst, d_z[1 if f == 0 else 7]))
+        return following
+
+    def ring_total(p, r, rows, half):
+        return (
+            p[z, half, rows, :].astype(F32) + r[half, 3, rows, :].astype(F32) + r[1 - half, 6, rows, :].astype(F32)
+        )
+
     l_subs = [pl.ds(0, 48), pl.ds(48, 48)]
     c_gu.wait()
     c_dn.wait()
     ffn_early(0)
-    e_ring = ring_start(ep, re, e_subs)
+    e_far = ring_begin(ep, re, True)
     norm_early(1)
     ffn_early(1)
+    e_near = ring_begin(ep, re, False)
+    fetch(3, 4)
     for copy in wz:
         copy.wait_recv()
     wz = [send(unit(7), unit(7), d_z[1]), send(unit(1), unit(1), d_z[7])]
-    ring_step(0, e_ring, ep, re, e_subs)
     norm_early(2)
     ffn_early(2)
     for copy in wz:
         copy.wait_recv()
     wz = [send(unit(6), unit(6), d_z[1]), send(unit(2), unit(2), d_z[7])]
-    ring_step(1, e_ring, ep, re, e_subs)
+    e_far = ring_next(e_far, ep, re, 0, 3, True)
+    fetch(5)
     norm_early(3)
     ffn_early(3)
     for copy in wz:
         copy.wait_recv()
     wz = [send(unit(5), unit(5), d_z[1])]
-    ring_step(2, e_ring, ep, re, e_subs)
 
     def prepare_late(j):
         for chunk in chunks(j):
@@ -197,34 +222,54 @@
     def slab(xx, cols):
         return w.at[xx, :, c, :, :, cols]
 
-    def core_half(cols):
-        return w.at[:, :, c, :, :, cols]
-
-    def same(piece, device):
-        return send(piece, piece, device)
-
     wa1 = [same(block(x, y, col_a), d) for d in (d_xp, d_xm)]
-    wb1 = [same(block(x, y, col_b), d) for d in (d_yp, d_ym)]
-    ring_step(3, e_ring, ep, re, e_subs)
+    e_near = ring_next(e_near, ep, re, 4, 2, False)
+    forward(0)
     prepare_late(1)
+    e_far = ring_next(e_far, ep, re, 1, 2, True)
+    forward(1, 2)
     wa1[0].wait_recv()
     wa1r = [same(block(xm, y, a_l), d_xp)]
     wa1[1].wait_recv()
     wa1r.append(same(block(xp, y, a_r), d_xm))
-    forwards = []
-    for s, copy in ((0, f_gu[0]), (1, f_gu[1])):
-        copy.wait_recv()
-        forwards.append(same(quarter(gux, s, c, 384, True), d_co))
-    ring_step(4, e_ring, ep, re, e_subs)
     prepare_late(2)
+    e_near = ring_next(e_near, ep, re, 5, 1, False)
+    forward(3)
+    prepare_late(3)
+    e_far = ring_next(e_far, ep, re, 2, 1, True)
     for copy in wa1r:
         copy.wait_recv()
-    wa2 = [same(column(y, col_a), d) for d in (d_yp, d_ym)]
-    ring_step(5, e_ring, ep, re, e_subs)
-    prepare_late(3)
-    for s, copy in ((0, f_dn[0]), (1, f_dn[1])):
-        copy.wait_recv()
-        forwards.append(same(quarter(dnx, s, c, 64, False), d_co))
+    forward(4, 5)
+    wb1 = [same(block(x, y, col_b), d) for d in (d_yp, d_ym)]
+
+    def main_a(k):
+        return [same(block(k, y, col_a), d) for d in (d_yp, d_ym)]
+
+    def relay_a(copies, k):
+        copies[0].wait_recv()
+        first = same(block(k, ym, a_l), d_yp)
+        copies[1].wait_recv()
+        return [first, same(block(k, yp, a_r), d_ym)]
+
+    def half_slab(xx, k, cols):
+        return w.at[xx, k, c, :, :, cols]
+
+    def main_b(k):
+        return [same(half_slab(x, k, col_b), d) for d in (d_xp, d_xm)]
+
+    def relay_b(copies, k):
+        copies[0].wait_recv()
+        first = same(half_slab(xm, k, b_l), d_xp)
+        copies[1].wait_recv()
+        return [first, same(half_slab(xp, k, b_r), d_xm)]
+
+    def done(*groups):
+        for copies in groups:
+            for copy in copies:
+                copy.wait_recv()
+
+    wa2 = [main_a(0)]
+    c_dho = send(dh_hbm, dho, d_co)
     for copy in forwards:
         copy.wait_recv()
 
@@ -242,27 +287,30 @@
             lp[cb, n // 2, :, cols] = out[LATE:]
 
     ffn_late(0)
-    l_ring = ring_start(lp, rl, l_subs)
-    for pair in e_ring:
-        for copy in pair:
-            copy.wait_recv()
+    l_far = ring_begin(lp, rl, True)
+    ffn_late(1)
+    l_near = ring_begin(lp, rl, False)
+    for copy in e_near + e_far:
+        copy.wait_recv()
     for d in range(2):
-        es[d] = (re[d, 6, e_subs[1], :].astype(F32) + ep[z, d, e_subs[1], :].astype(F32)).astype(BF16)
+        es[d] = ring_total(ep, re, pl.ds(EARLY, EARLY), d).astype(BF16)
     c_ex = send(es, ex, d_pair)
     wb1[0].wait_recv()
     wb1r = [same(block(x, ym, b_l), d_yp)]
     wb1[1].wait_recv()
     wb1r.append(same(block(x, yp, b_r), d_ym))
-
-    @pl.loop(1, 3)
+    wa2.append(main_a(1))
+
+    @pl.loop(2, 4)
     def _(j):
         ffn_late(j)
 
-    for copy in wb1r:
-        copy.wait_recv()
-    wb2 = [same(slab(x, col_b), d) for d in (d_xp, d_xm)]
-    ffn_late(3)
-    ring_step(0, l_ring, lp, rl, l_subs)
+    l_far = ring_next(l_far, lp, rl, 0, 3, True)
+    done(wb1r)
+    wb2 = [main_b(0)]
+    wa2.append(main_a(2))
+    wa2r = [relay_a(wa2[0], 0)]
+    w_co = [same(column(y, col_a), d_co), same(slab(x, col_b), d_co)]
     c_dh.wait()
     c_dho.wait_recv()
 
@@ -277,27 +325,22 @@
                         turned[low * 64:(low + 1) * 64]
                     )
 
-    ring_step(1, l_ring, lp, rl, l_subs)
-    wa2[0].wait_recv()
-    wa2r = [same(column(ym, a_l), d_yp)]
-    wa2[1].wait_recv()
-    wa2r.append(same(column(yp, a_r), d_ym))
-    ring_step(2, l_ring, lp, rl, l_subs)
-    wb2[0].wait_recv()
-    wb2r = [same(slab(xm, b_l), d_xp)]
-    wb2[1].wait_recv()
-    wb2r.append(same(slab(xp, b_r), d_xm))
-    ring_step(3, l_ring, lp, rl, l_subs)
-    for copy in wa2r:
-        copy.wait_recv()
-    w_co = [same(core_half(col_a), d_co)]
-    ring_step(4, l_ring, lp, rl, l_subs)
-    for copy in wb2r:
-        copy.wait_recv()
-    w_co.append(same(core_half(col_b), d_co))
-    ring_step(5, l_ring, lp, rl, l_subs)
-    for copy in w_co:
-        copy.wait_recv()
+    l_near = ring_next(l_near, lp, rl, 4, 2, False)
+    wb2.append(main_b(1))
+    wa2.append(main_a(3))
+    wa2r.append(relay_a(wa2[1], 1))
+    l_far = ring_next(l_far, lp, rl, 1, 2, True)
+    wb2r = [relay_b(wb2[0], 0)]
+    wa2r.append(relay_a(wa2[2], 2))
+    l_near = ring_next(l_near, lp, rl, 5, 1, False)
+    wb2r.append(relay_b(wb2[1], 1))
+    wa2r.append(relay_a(wa2[3], 3))
+    w_co += [same(column(yy, col_a), d_co) for yy in (ym, yp)]
+    w_co += [same(slab(xx, col_b), d_co) for xx in (xm, xp)]
+    l_last = ring_next(l_far, lp, rl, 2, 1, True, l_subs)
+    done(*wa2r, *wb2r)
+    w_co += [same(column(y2, col_a), d_co), same(slab(x2, col_b), d_co)]
+    done(w_co)
 
     @pl.loop(0, 3)
     def _(n):
@@ -335,21 +378,20 @@
     @pl.loop(0, EARLY // 16)
     def _(i):
         rows = pl.ds(pl.multiple_of(i * 16, 16), 16)
-        branch = [
-            ep[z, d, rows, :].astype(F32) + re[d, 6, rows, :].astype(F32) + ex[d, rows, :].astype(F32)
-            for d in range(2)
-        ]
+        branch = [ring_total(ep, re, rows, d) + ex[d, rows, :].astype(F32) for d in range(2)]
         loss_gradient(xs[yl * 8 + z, rows, :], branch, rows)
 
     c_gp = [swap_gradient(0, EARLY)]
+    for copy in l_near:
+        copy.wait_recv()
     for k in range(2):
-        for d in range(2):
-            l_ring[k][d].wait_recv()
+        l_last[k].wait_recv()
+        l_last[k + 2].wait_recv()
 
         @pl.loop(3 * k, 3 * k + 3)
         def _(i):
             rows = pl.ds(pl.multiple_of(i * 16, 16), 16)
-            branch = [lp[z, d, rows, :].astype(F32) + rl[d, 6, rows, :].astype(F32) for d in range(2)]
+            branch = [ring_total(lp, rl, rows, d) for d in range(2)]
             loss_gradient(xl[z, rows, :], branch, pl.ds(pl.multiple_of(EARLY + i * 16, 16), 16))
 
         c_gp.append(swap_gradient(EARLY + 48 * k, 48))

time: 111 us -> 104 us (0.937)
  Pallas kernels: 107 us -> 99.5 us
    pallas_call x1, Pallas kernels: 107 us -> 99.5 us  [on_device(): pl.pallas_call(kernel, out_shape=(jax.ShapeDtypeStruct((1, TOKENS, WIDTH)...]
where the time goes in v3:
time: 104 us; the launch traced here: 103 us
  Pallas kernels  99.5 us (96%)
  local copies, waits for them, and re-layouts  3.3 us (3%)
    pallas_call x1, Pallas kernels, on_device(): pl.pallas_call(kernel, out_shape=(jax.ShapeDtypeStruct((1, TOKENS, WIDTH)...  99.5 us
    unnamed x2, local copies, waits for them, and re-layouts  3.3 us

profile of v3, /device:TPU:1, one launch (start us, length us, event | category | flops | bytes accessed | tf_op | source)
XLA Modules:
  0.0 103.4 jit_solution(2038970243187687690)
XLA Ops:
  0.6 99.5 %shard_map.113 = (bf16[1,128,2048]{2,1,0:T(8,128)(2,1)}, f32[8,1536]{1,0:T(8,128)}) custom-call(bf16[16,128,1536]{2,1,0:T(8,128)(2,1)} %bitcast.2, f32[1536]{0:T(1024)} %g1_ref.1, f32[1536]{0:T(1024)} %b1_ref.1, bf16[2,1536,256]{2,1,0:T(8,128)(2,1)} %gu_hbm.1, bf16[256,1536]{1,0:T(8,128)(2,1)} %dn_hbm.1, f32[1536]{0:T(1024)} %ls_ref.1, f32[1536]{0:T(1024)} %g2_ref.1, ...), custom_call_target="tpu_custom_call" | custom-call | tf_op jit(solution)/shard_map/pallas_call | solution.py:507
  100.1 1.9 %copy.14 = bf16[1,128,2048]{2,1,0:T(8,128)(2,1)} copy(bf16[1,128,2048]{2,1,0:T(8,128)(2,1)} %get-tuple-element.4) | data formatting | bytes 1048576
  102.0 1.4 %copy.15 = f32[8,1536]{1,0:T(8,128)} copy(f32[8,1536]{1,0:T(8,128)} %get-tuple-element.5) | data formatting | bytes 98304

commit v4 on v3

--- a/solution.py
+++ b/solution.py
@@ -436,9 +436,9 @@
     oa = first(ga, ra, x2, *on_x)
     grad_slab(xp)
     grad_slab(xm)
-    second(oa, ga, ra, *on_x)
     grad_slab(x)
     ob = first(gb, rb, y2, *on_y)
+    second(oa, ga, ra, *on_x)
     second(ob, gb, rb, *on_y)
 
     def hidden_gradient(k):
@@ -484,6 +484,8 @@
         s3[:, :, pl.ds(k * Q, Q)] = both.astype(BF16)
     last = [send(s3.at[(z + k) % 8], r3.at[z], d_z[k]) for k in (4, 3, 5, 2, 6, 1, 7)]
     r3[z] = s3[z]
+    for copy in sent[:-7]:
+        copy.wait_send()
     for copy in last:
         copy.wait_recv()
     tot = jnp.sum(r3[...].astype(F32), axis=0) * (1.0 / (16 * 2048) ** 0.5)
@@ -491,7 +493,7 @@
     res[1] = tot[8:]
     c_fin = send(res.at[1 - c], fin, d_co)
     gw_ref[:, pl.ds(pl.multiple_of(c * H, H), H)] = res[c]
-    for copy in sent[:-1]:
+    for copy in last:
         copy.wait_send()
     c_fin.wait_recv()
     gw_ref[:, pl.ds(pl.multiple_of((1 - c) * H, H), H)] = fin[...]

time: 104 us -> 104 us (level)
  no operation moved by 1% of the time
where the time goes in v4:
time: 104 us; the launch traced here: 103 us
  Pallas kernels  99.4 us (96%)
  local copies, waits for them, and re-layouts  3.3 us (3%)
    pallas_call x1, Pallas kernels, on_device(): pl.pallas_call(kernel, out_shape=(jax.ShapeDtypeStruct((1, TOKENS, WIDTH)...  99.4 us
    unnamed x2, local copies, waits for them, and re-layouts  3.3 us

profile of v4, /device:TPU:1, one launch (start us, length us, event | category | flops | bytes accessed | tf_op | source)
XLA Modules:
  0.0 103.4 jit_solution(10894713962824914518)
XLA Ops:
  0.6 99.4 %shard_map.113 = (bf16[1,128,2048]{2,1,0:T(8,128)(2,1)}, f32[8,1536]{1,0:T(8,128)}) custom-call(bf16[16,128,1536]{2,1,0:T(8,128)(2,1)} %bitcast.2, f32[1536]{0:T(1024)} %g1_ref.1, f32[1536]{0:T(1024)} %b1_ref.1, bf16[2,1536,256]{2,1,0:T(8,128)(2,1)} %gu_hbm.1, bf16[256,1536]{1,0:T(8,128)(2,1)} %dn_hbm.1, f32[1536]{0:T(1024)} %ls_ref.1, f32[1536]{0:T(1024)} %g2_ref.1, ...), custom_call_target="tpu_custom_call" | custom-call | tf_op jit(solution)/shard_map/pallas_call | solution.py:509
  100.1 1.9 %copy.14 = bf16[1,128,2048]{2,1,0:T(8,128)(2,1)} copy(bf16[1,128,2048]{2,1,0:T(8,128)(2,1)} %get-tuple-element.4) | data formatting | bytes 1048576
  102.0 1.4 %copy.15 = f32[8,1536]{1,0:T(8,128)} copy(f32[8,1536]{1,0:T(8,128)} %get-tuple-element.5) | data formatting | bytes 98304
